TPU v7x, 32 devices: a whole 2x2x4 slice. The times are simulated.
32 devices in a mesh: grp: 16 (over z, y, x), fold: 2 (over core).
Axes of the slice: x: 2, y: 2, z: 4, core: 2. Of those that a mesh axis runs over, the one named last changes fastest.
Arguments:
- blocks: bfloat16 [9, 2, 64, 64, 2048], P(None, None, 'fold', None, 'grp'), may hold values from -30 to 30
- source: bfloat16 [2, 64, 12, 2048], P(None, 'fold', None, 'grp'), may hold values from -8 to 8
- plane_counts: int32 [16], P('grp'), may hold values from 1 to 2, 24 in all
Outputs:
- solution: float32 [2, 64, 12, 2048], P(None, 'fold', None, 'grp')
- residual: float32 [2, 64, 12, 2048], P(None, 'fold', None, 'grp')
Inputs may be any that keep to these rules, and one draw needn't show every extreme that they name: plane_counts sum to 24; the busiest group holds exactly 2 planes.
All inputs are finite; a program needn't handle non-finite values.
Results may differ from a plain program's by a relative error of at most 0.0032.
Values may be sent and summed in bfloat16 or wider, within the bound.
A program may use at most 128 MiB of HBM per device.

v0:
```python
import jax
import jax.numpy as jnp
from jax import lax
from jax.sharding import PartitionSpec as P

LX = 4
LY = 4
LT = 4
SWEEPS = 2


def extended_2(array, sides, width):
    for axis, dim in sides:
        devices, length = (lax.axis_size(axis), array.shape[dim])
        up = [(i, (i + 1) % devices) for i in range(devices)]
        down = [(j, i) for i, j in up]
        last = lax.slice_in_dim(array, length - width, length, axis=dim)
        first = lax.slice_in_dim(array, 0, width, axis=dim)
        before = lax.ppermute(last, axis, up)
        after = lax.ppermute(first, axis, down)
        array = jnp.concatenate([before, array, after], axis=dim)
    return array


def stencil_apply(blocks, neighbours):
    stacked = jnp.stack(neighbours)
    swapped = jnp.stack([-stacked[:, 1], stacked[:, 0]], axis=1)
    operand = jnp.stack([stacked, swapped], axis=1)
    return jnp.einsum("mjrcs,mjpcks->prks", blocks, operand, preferred_element_type=jnp.float32)


def end_planes(vector, owned_count, plane_sites):
    first_plane = vector[..., :plane_sites]
    last_plane = lax.dynamic_slice_in_dim(vector, (owned_count - 1) * plane_sites, plane_sites, 3)
    return jnp.concatenate([first_plane, last_plane], axis=3)


def attach_rims(vector, with_rims, owned_count, plane_sites):
    previous = with_rims[..., :plane_sites]
    following = with_rims[..., 3 * plane_sites :]
    padding = jnp.zeros_like(previous)
    extended = jnp.concatenate([previous, vector, padding], axis=3)
    return lax.dynamic_update_slice_in_dim(extended, following, (owned_count + 1) * plane_sites, 3)


def hop_vectors(extended, plane_sites):
    leading = extended.shape[:3]
    capacity = extended.shape[3] // plane_sites - 2
    flat_shape = leading + (capacity * plane_sites,)
    by_plane = extended.reshape(leading + (capacity + 2, plane_sites))
    center = by_plane[:, :, :, 1 : capacity + 1]
    lower_plane = by_plane[:, :, :, :capacity].reshape(flat_shape)
    upper_plane = by_plane[:, :, :, 2:].reshape(flat_shape)
    lattice = center.reshape(leading + (capacity, LX, LY, LT))
    neighbours = [center.reshape(flat_shape)]
    for axis_index in (4, 5):
        neighbours.append(jnp.roll(lattice, -1, axis_index).reshape(flat_shape))
        neighbours.append(jnp.roll(lattice, 1, axis_index).reshape(flat_shape))
    neighbours.append(upper_plane)
    neighbours.append(lower_plane)
    neighbours.append(jnp.roll(lattice, -1, 6).reshape(flat_shape))
    neighbours.append(jnp.roll(lattice, 1, 6).reshape(flat_shape))
    return neighbours


def body(blocks, source, plane_counts):
    plane_sites = LX * LY * LT
    owned_count = plane_counts[0]
    site_total = source.shape[3]
    live_mask = (jnp.arange(site_total) // plane_sites < owned_count).astype(jnp.float32)
    residual = source.astype(jnp.float32) * live_mask
    solution = jnp.zeros_like(residual)
    for sweep_index in range(SWEEPS):
        rounded = residual.astype(jnp.bfloat16)
        gathered = lax.all_gather(rounded, "fold", axis=1, tiled=True)
        with_rims = extended_2(
            end_planes(gathered, owned_count, plane_sites), (("grp", 3),), plane_sites
        )
        extended = attach_rims(gathered, with_rims, owned_count, plane_sites)
        neighbours = hop_vectors(extended, plane_sites)
        applied = stencil_apply(blocks, neighbours) * live_mask
        intersection_re = jnp.sum(applied[0] * residual[0] + applied[1] * residual[1], axis=(0, 2))
        intersection_im = jnp.sum(applied[0] * residual[1] - applied[1] * residual[0], axis=(0, 2))
        image_norm = jnp.sum(applied * applied, axis=(0, 1, 3))
        intersection_re, intersection_im, image_norm = lax.psum(
            (intersection_re, intersection_im, image_norm), ("grp", "fold")
        )
        alpha_re = (intersection_re / image_norm)[:, None]
        alpha_im = (intersection_im / image_norm)[:, None]
        solution = solution + jnp.stack(
            [
                alpha_re * residual[0] - alpha_im * residual[1],
                alpha_re * residual[1] + alpha_im * residual[0],
            ]
        )
        residual = residual - jnp.stack(
            [
                alpha_re * applied[0] - alpha_im * applied[1],
                alpha_re * applied[1] + alpha_im * applied[0],
            ]
        )
    return (solution, residual)


def solution(mesh):
    return jax.shard_map(
        body,
        mesh=mesh,
        in_specs=(P(None, None, "fold", None, "grp"), P(None, "fold", None, "grp"), P("grp")),
        out_specs=(P(None, "fold", None, "grp"), P(None, "fold", None, "grp")),
        check_vma=False,
    )
```

profile of v0, /device:TPU:0, one launch (start us, length us, event | category | flops | bytes accessed | tf_op | source)
XLA Modules:
  0.0 251.9 jit_solution(14557403301665931129)
XLA Ops:
  1.3 1.0 fusion.14
  2.5 2.2 all_gather.6
  5.4 2.9 %collective-permute-start = (bf16[2,64,12,64]{3,0,2,1:T(2,128)(2,1)S(1)}, bf16[2,64,12,64]{3,0,2,1:T(2,128)(2,1)S(1)}, u32[]{:S(2)}, u32[]{:S(2)}) collective-permute-start(bf16[2,64,12,64]{3,0,2,1:T(2,128)(2,1)S(1)} %get-tuple-element.75), channel_id=1, source_target_pairs={{0,2},{2,4},{4,6},{6,8},{8,10},{10,12},{12,14},{14,16},{16,18},{18... | collective-permute-start | bytes 589832 | tf_op jit(solution)/shard_map/ppermute | solution.py:19
  8.3 4.1 %collective-permute-start.1 = (bf16[2,64,12,64]{3,0,2,1:T(2,128)(2,1)S(1)}, bf16[2,64,12,64]{3,0,2,1:T(2,128)(2,1)S(1)}, u32[]{:S(2)}, u32[]{:S(2)}) collective-permute-start(bf16[2,64,12,64]{3,0,2,1:T(2,128)(2,1)S(1)} %get-tuple-element.74), channel_id=1, source_target_pairs={{2,0},{4,2},{6,4},{8,6},{10,8},{12,10},{14,12},{16,14},{18,16},{20... | collective-permute-start | bytes 589832 | tf_op jit(solution)/shard_map/ppermute | solution.py:20
  12.4 26.7 %copy.242 = bf16[9,2,32,64,128,1]{3,2,0,1,5,4:T(8,128)(2,1)} copy(bf16[9,2,32,64,128,1]{4,3,2,1,0,5:T(8,128)(2,1)} %bitcast.70) | data formatting | bytes 18874368 | tf_op args[0]
  39.9 3.0 %dynamic_update_slice.6 = bf16[2,64,12,256]{3,1,2,0:T(8,128)(2,1)S(1)} dynamic-update-slice(bf16[2,64,12,256]{3,1,2,0:T(8,128)(2,1)S(1)} %maximum_maximum_fusion, bf16[2,64,12,64]{3,1,2,0:T(8,128)(2,1)S(1)} %copy.211, s32[]{:T(128)} %constant.22.clone.1, s32[]{:T(128)} %constant.22.clone.1, s32[]{:T(128)} %constant.22.clone.1, s32[]{:T(128)S(6)} %select_n.19) | dynamic-update-slice | bytes 393220 | tf_op jit(solution)/shard_map/dynamic_update_slice | solution.py:43
  42.9 1.0 copy.212
  46.9 1.0 fusion.27
  49.2 1.2 pad_maximum_fusion
  51.7 1.3 pad_maximum_fusion.2
  54.6 2.4 pad_maximum_fusion.4
  58.3 4.9 %slice_negate_fusion.1 = (bf16[9,1,64,12,128]{2,3,0,1,4:T(8,128)(2,1)}, bf16[9,1,64,12,128]{2,3,0,1,4:T(8,128)(2,1)}) fusion(bf16[9,2,64,12,128]{2,3,0,1,4:T(8,128)(2,1)S(1)} %copy_dynamic-update-slice_fusion.6), kind=kLoop, calls=%fused_computation.11 | loop fusion | flops 884736 | bytes 7077888 | tf_op jit(solution)/shard_map/neg | solution.py:27
  63.1 1.6 copy-done.1
  64.7 9.6 %maximum_bitcast_fusion = bf16[9,1,2,64,12,128]{3,4,0,1,2,5:T(8,128)(2,1)} fusion(bf16[9,1,64,12,128]{2,3,0,1,4:T(8,128)(2,1)} %get-tuple-element.33, bf16[9,1,64,12,128]{2,3,0,1,4:T(8,128)(2,1)} %get-tuple-element.32), kind=kLoop, calls=%fused_computation.8 | loop fusion | flops 1769472 | bytes 7077888 | tf_op jit(solution)/shard_map/stack | solution.py:28
  74.3 14.1 %fusion.11 = f32[128,2,12,32]{3,2,1,0:T(8,128)S(1)} fusion(bf16[9,2,32,64,128,1]{3,2,0,1,5,4:T(8,128)(2,1)} %copy.242, bf16[9,1,2,64,12,128]{3,4,0,1,2,5:T(8,128)(2,1)} %maximum_bitcast_fusion, bf16[9,1,2,64,12,128]{3,4,0,1,2,5:T(8,128)(2,1)} %bitcast.67), kind=kOutput, calls=%fused_computation.13 | convolution fusion | flops 230031360 | bytes 16908288 | tf_op jit(solution)/shard_map/mjrcs,mjpcks->prks/dot_general | solution.py:29
  88.4 1.0 copy.224
  89.8 41.4 %all-reduce.1 = (f32[12]{0:T(128)S(1)}, f32[12]{0:T(128)S(1)}, f32[12]{0:T(128)S(1)}) all-reduce(f32[12]{0:T(128)S(1)} %get-tuple-element.17, f32[12]{0:T(128)S(1)} %get-tuple-element.28, f32[12]{0:T(128)S(1)} %get-tuple-element.16), channel_id=1, replica_groups=mesh['grp'=16,'fold'=2] {'grp','fold'}, use_global_device_ids=true, to_apply=%region_5.6 | all-reduce | flops 36 | bytes 288 | tf_op jit(solution)/shard_map/psum | solution.py:85
  132.4 2.1 all_gather.7
  135.2 2.3 collective-permute-start.2
  137.7 3.4 %collective-permute-start.3 = (bf16[2,64,12,64]{3,0,2,1:T(2,128)(2,1)S(1)}, bf16[2,64,12,64]{3,0,2,1:T(2,128)(2,1)S(1)}, u32[]{:S(2)}, u32[]{:S(2)}) collective-permute-start(bf16[2,64,12,64]{3,0,2,1:T(2,128)(2,1)S(1)} %get-tuple-element.72), channel_id=1, source_target_pairs={{2,0},{4,2},{6,4},{8,6},{10,8},{12,10},{14,12},{16,14},{18,16},{20... | collective-permute-start | bytes 589832 | tf_op jit(solution)/shard_map/ppermute | solution.py:20
  141.0 13.6 %collective-permute-done.2 = bf16[2,64,12,64]{3,0,2,1:T(2,128)(2,1)S(1)} collective-permute-done((bf16[2,64,12,64]{3,0,2,1:T(2,128)(2,1)S(1)}, bf16[2,64,12,64]{3,0,2,1:T(2,128)(2,1)S(1)}, u32[]{:S(2)}, u32[]{:S(2)}) %collective-permute-start.2) | collective-permute-done | bytes 196640 | tf_op jit(solution)/shard_map/ppermute | solution.py:19
  155.2 1.4 collective-permute-done.3
  156.7 3.0 %dynamic_update_slice.7 = bf16[2,64,12,256]{3,1,2,0:T(8,128)(2,1)S(1)} dynamic-update-slice(bf16[2,64,12,256]{3,1,2,0:T(8,128)(2,1)S(1)} %maximum_maximum_fusion.1, bf16[2,64,12,64]{3,1,2,0:T(8,128)(2,1)S(1)} %copy.228, s32[]{:T(128)} %constant.22.clone.1, s32[]{:T(128)} %constant.22.clone.1, s32[]{:T(128)} %constant.22.clone.1, s32[]{:T(128)S(6)} %select_n.19) | dynamic-update-slice | bytes 393220 | tf_op jit(solution)/shard_map/dynamic_update_slice | solution.py:43
  159.7 1.0 copy.229
  168.4 1.0 pad_maximum_fusion.11
  169.4 1.0 pad_maximum_fusion.10
  174.8 4.9 %slice_negate_fusion = (bf16[9,1,64,12,128]{2,3,0,1,4:T(8,128)(2,1)}, bf16[9,1,64,12,128]{2,3,0,1,4:T(8,128)(2,1)}) fusion(bf16[9,2,64,12,128]{2,3,0,1,4:T(8,128)(2,1)S(1)} %copy_dynamic-update-slice_fusion), kind=kLoop, calls=%fused_computation.10 | loop fusion | flops 884736 | bytes 7077888 | tf_op jit(solution)/shard_map/neg | solution.py:27
  179.6 1.6 copy-done
  181.2 9.6 %maximum_bitcast_fusion.1 = bf16[9,1,2,64,12,128]{3,4,0,1,2,5:T(8,128)(2,1)} fusion(bf16[9,1,64,12,128]{2,3,0,1,4:T(8,128)(2,1)} %get-tuple-element.31, bf16[9,1,64,12,128]{2,3,0,1,4:T(8,128)(2,1)} %get-tuple-element.30), kind=kLoop, calls=%fused_computation.9 | loop fusion | flops 1769472 | bytes 7077888 | tf_op jit(solution)/shard_map/stack | solution.py:28
  190.8 14.2 %fusion.8 = f32[128,2,12,32]{3,2,1,0:T(8,128)S(1)} fusion(bf16[9,2,32,64,128,1]{3,2,0,1,5,4:T(8,128)(2,1)} %copy.242, bf16[9,1,2,64,12,128]{3,4,0,1,2,5:T(8,128)(2,1)} %maximum_bitcast_fusion.1, bf16[9,1,2,64,12,128]{3,4,0,1,2,5:T(8,128)(2,1)} %bitcast.66), kind=kOutput, calls=%fused_computation.12 | convolution fusion | flops 230031360 | bytes 16908288 | tf_op jit(solution)/shard_map/mjrcs,mjpcks->prks/dot_general | solution.py:29
  205.1 1.0 copy.241
  206.4 43.4 %all-reduce = (f32[12]{0:T(128)S(1)}, f32[12]{0:T(128)S(1)}, f32[12]{0:T(128)S(1)}) all-reduce(f32[12]{0:T(128)S(1)} %get-tuple-element.15, f32[12]{0:T(128)S(1)} %get-tuple-element.24, f32[12]{0:T(128)S(1)} %get-tuple-element.14), channel_id=1, replica_groups=mesh['grp'=16,'fold'=2] {'grp','fold'}, use_global_device_ids=true, to_apply=%region_11.12 | all-reduce | flops 36 | bytes 288 | tf_op jit(solution)/shard_map/psum | solution.py:85
  (77 shorter events, 26.8 us)
Async XLA Ops:
  5.4 33.9 %collective-permute-start = (bf16[2,64,12,64]{3,0,2,1:T(2,128)(2,1)S(1)}, bf16[2,64,12,64]{3,0,2,1:T(2,128)(2,1)S(1)}, u32[]{:S(2)}, u32[]{:S(2)}) collective-permute-start(bf16[2,64,12,64]{3,0,2,1:T(2,128)(2,1)S(1)} %get-tuple-element.75), channel_id=1, source_target_pairs={{0,2},{2,4},{4,6},{6,8},{8,10},{10,12},{12,14},{14,16},{16,18},{18... | collective-permute-start | bytes 589832 | tf_op jit(solution)/shard_map/ppermute | solution.py:19
  8.3 31.5 %collective-permute-start.1 = (bf16[2,64,12,64]{3,0,2,1:T(2,128)(2,1)S(1)}, bf16[2,64,12,64]{3,0,2,1:T(2,128)(2,1)S(1)}, u32[]{:S(2)}, u32[]{:S(2)}) collective-permute-start(bf16[2,64,12,64]{3,0,2,1:T(2,128)(2,1)S(1)} %get-tuple-element.74), channel_id=1, source_target_pairs={{2,0},{4,2},{6,4},{8,6},{10,8},{12,10},{14,12},{16,14},{18,16},{20... | collective-permute-start | bytes 589832 | tf_op jit(solution)/shard_map/ppermute | solution.py:20
  58.3 6.4 %copy-start.1 = (bf16[9,2,64,12,128]{2,3,0,1,4:T(8,128)(2,1)}, bf16[9,2,64,12,128]{2,3,0,1,4:T(8,128)(2,1)S(1)}, u32[]{:S(2)}) copy-start(bf16[9,2,64,12,128]{2,3,0,1,4:T(8,128)(2,1)S(1)} %copy_dynamic-update-slice_fusion.6) | copy-start | bytes 10616836
  74.3 57.9 %copy-start.4 = (bf16[2,32,12,128]{3,1,2,0:T(8,128)(2,1)S(1)}, bf16[2,32,12,128]{3,1,2,0:T(8,128)(2,1)}, u32[]{:S(2)}) copy-start(bf16[2,32,12,128]{3,1,2,0:T(8,128)(2,1)} %param.4) | copy-start | bytes 589828
  135.2 19.4 %collective-permute-start.2 = (bf16[2,64,12,64]{3,0,2,1:T(2,128)(2,1)S(1)}, bf16[2,64,12,64]{3,0,2,1:T(2,128)(2,1)S(1)}, u32[]{:S(2)}, u32[]{:S(2)}) collective-permute-start(bf16[2,64,12,64]{3,0,2,1:T(2,128)(2,1)S(1)} %get-tuple-element.73), channel_id=1, source_target_pairs={{0,2},{2,4},{4,6},{6,8},{8,10},{10,12},{12,14},{14,16},{16,18},{18... | collective-permute-start | bytes 589832 | tf_op jit(solution)/shard_map/ppermute | solution.py:19
  137.7 18.9 %collective-permute-start.3 = (bf16[2,64,12,64]{3,0,2,1:T(2,128)(2,1)S(1)}, bf16[2,64,12,64]{3,0,2,1:T(2,128)(2,1)S(1)}, u32[]{:S(2)}, u32[]{:S(2)}) collective-permute-start(bf16[2,64,12,64]{3,0,2,1:T(2,128)(2,1)S(1)} %get-tuple-element.72), channel_id=1, source_target_pairs={{2,0},{4,2},{6,4},{8,6},{10,8},{12,10},{14,12},{16,14},{18,16},{20... | collective-permute-start | bytes 589832 | tf_op jit(solution)/shard_map/ppermute | solution.py:20
  174.8 6.4 %copy-start = (bf16[9,2,64,12,128]{2,3,0,1,4:T(8,128)(2,1)}, bf16[9,2,64,12,128]{2,3,0,1,4:T(8,128)(2,1)S(1)}, u32[]{:S(2)}) copy-start(bf16[9,2,64,12,128]{2,3,0,1,4:T(8,128)(2,1)S(1)} %copy_dynamic-update-slice_fusion) | copy-start | bytes 10616836
  190.8 60.0 %copy-start.2 = (f32[1,32,12,128]{3,1,2,0:T(8,128)S(1)}, f32[1,32,12,128]{3,1,2,0:T(8,128)}, u32[]{:S(2)}) copy-start(f32[1,32,12,128]{3,1,2,0:T(8,128)} %get-tuple-element.80) | copy-start | bytes 589828
  190.8 60.0 %copy-start.3 = (f32[1,32,12,128]{3,1,2,0:T(8,128)S(1)}, f32[1,32,12,128]{3,1,2,0:T(8,128)}, u32[]{:S(2)}) copy-start(f32[1,32,12,128]{3,1,2,0:T(8,128)} %get-tuple-element.81) | copy-start | bytes 589828
where the time goes:
time: 256 us; the launch traced here: 252 us
  blocking collectives  89.1 us (35%)
  local copies, waits for them, and re-layouts  61 us (24%)
  other arithmetic  43.7 us (17%)
  matrix products  28.3 us (11%)
  waiting for transfers between devices  15 us (6%)
  starting transfers between devices  12.7 us (5%)
    psum x2, blocking collectives, body(): lax.psum((intersection_re, intersection_im, image_norm), ('grp', 'fold'))  84.8 us
    unnamed x27, local copies, waits for them, and re-layouts  37.3 us
    dot_general x2, matrix products, stencil_apply(): jnp.einsum('mjrcs,mjpcks->prks', blocks, operand, preferred_element_type=...  28.3 us
    another operation x2, other arithmetic, stencil_apply(): operand = jnp.stack([stacked, swapped], axis=1)  19.2 us
    ppermute x2, waiting for transfers between devices, extended_2(): before = lax.ppermute(last, axis, up)  13.6 us
    neg x2, other arithmetic, stencil_apply(): swapped = jnp.stack([-stacked[:, 1], stacked[:, 0]], axis=1)  9.73 us
    dynamic_update_slice x4, local copies, waits for them, and re-layouts, attach_rims(): lax.dynamic_update_slice_in_dim(extended, following, (owned_count + 1) *...  8.15 us
    ppermute x2, starting transfers between devices, extended_2(): after = lax.ppermute(first, axis, down)  7.46 us
  transfers between devices with their start and end apart: 4, of which 2 were waited for; matrix products, arithmetic and copies ran while one was open for 11% of the time, Pallas kernels for 0%

commit v1 on v0

v1 whole, which is shorter than its diff:
```python
import functools

import jax
import jax.numpy as jnp
import numpy as np
from jax import lax
from jax.experimental import pallas as pl
from jax.experimental.pallas import tpu as pltpu
from jax.sharding import PartitionSpec as P

SWEEPS = 2
CHUNK = 8
GROUPS = 16
HALF = GROUPS // 2
LOCAL = (0, 1, 2, 3, 4, 7, 8)
ACROSS = (5, 6)
MESH = pl.DeviceIdType.MESH


def lane_moves():
    moves = np.zeros((256, 512), np.float32)
    for lane in range(128):
        base, site = lane // 8 * 8, lane % 8
        low = site < 4
        moves[base + (site ^ 4) + (0 if low else 128), lane] = 1
        moves[base + (site ^ 4) + (128 if low else 0), 128 + lane] = 1
        moves[base + (site & 4) + ((site + 1) & 3), 256 + lane] = 1
        moves[base + (site & 4) + ((site - 1) & 3), 384 + lane] = 1
    return jnp.asarray(moves, jnp.bfloat16)


def kernel(n_grp, n_fold, counts, blocks, source, moves, sol_out, res_out,
           raw, w_local, w_across, res, sol, image, gath, last, rims, local_rhs, red,
           load_sem, x_send, x_recv, r_send, r_recv, s_send, s_recv):
    bf16, f32 = jnp.bfloat16, jnp.float32
    rows, comps = blocks.shape[2], blocks.shape[3]
    nrhs = source.shape[1]
    total = n_grp * n_fold
    grp, fold = lax.axis_index("grp"), lax.axis_index("fold")
    me = grp * n_fold + fold
    loads = [pltpu.make_async_copy(blocks.at[m], raw.at[m], load_sem.at[m]) for m in range(9)]
    for load in loads:
        load.start()

    def device(index):
        return (lax.div(index, n_fold), lax.rem(index, n_fold))

    barrier = pltpu.get_barrier_semaphore()

    def greet(d, carry):
        pl.semaphore_signal(barrier, inc=1, device_id=device(lax.rem(me + d, total)), device_id_type=MESH)
        return carry

    lax.fori_loop(1, total, greet, 0)

    live = (counts[0] - 1).astype(f32)
    lane = lax.broadcasted_iota(jnp.int32, (rows, 128), 1)

    for p in range(2):
        planes = [source[p, k].astype(f32) for k in range(nrhs)]
        for g in range(GROUPS):
            value = jnp.zeros((rows, 128), f32)
            for k in range(nrhs):
                shift = 8 * (k - g) % 128
                moved = planes[k] if shift == 0 else pltpu.roll(planes[k], shift, 1)
                value = jnp.where(lane // 8 == k, moved, value)
            if g >= HALF:
                value = value * live
            res[g, :, 128 * p:128 * p + 128] = value

    pl.semaphore_wait(barrier, total - 1)

    def send_parts(sweep):
        def fill(h, carry):
            lower, upper = res[h], res[h + HALF]
            gath[sweep, fold, h] = lower.astype(bf16)
            gath[sweep, fold, h + HALF] = upper.astype(bf16)
            last[sweep, h] = (upper * live + lower * (1.0 - live)).astype(bf16)
            return carry

        lax.fori_loop(0, HALF, fill, 0)
        gathers, edges = [], []
        for d in range(1, n_fold):
            gathers.append(pltpu.make_async_remote_copy(
                src_ref=gath.at[sweep, fold], dst_ref=gath.at[sweep, fold],
                send_sem=x_send.at[sweep, d], recv_sem=x_recv.at[sweep, d],
                device_id=(grp, lax.rem(fold + d, n_fold)), device_id_type=MESH))
        for d in range(n_fold):
            other = lax.rem(fold + d, n_fold)
            edges.append(pltpu.make_async_remote_copy(
                src_ref=gath.at[sweep, fold, pl.ds(0, HALF)], dst_ref=rims.at[sweep, 0, fold],
                send_sem=r_send.at[sweep, 0, d], recv_sem=r_recv.at[sweep, 0, d],
                device_id=(lax.rem(grp + n_grp - 1, n_grp), other), device_id_type=MESH))
            edges.append(pltpu.make_async_remote_copy(
                src_ref=last.at[sweep], dst_ref=rims.at[sweep, 1, fold],
                send_sem=r_send.at[sweep, 1, d], recv_sem=r_recv.at[sweep, 1, d],
                device_id=(lax.rem(grp + 1, n_grp), other), device_id_type=MESH))
        for copy in gathers + edges:
            copy.start()
        return gathers, edges

    def wait_gather(sweep):
        for d in range(1, n_fold):
            sender = lax.rem(fold + n_fold - d, n_fold)
            slot = gath.at[sweep, sender]
            pltpu.make_async_remote_copy(
                src_ref=slot, dst_ref=slot, send_sem=x_send.at[sweep, d], recv_sem=x_recv.at[sweep, d],
                device_id=(grp, lax.rem(fold + d, n_fold)), device_id_type=MESH).wait_recv()

    def wait_edges(sweep):
        for side in range(2):
            for d in range(n_fold):
                sender = lax.rem(fold + n_fold - d, n_fold)
                slot = rims.at[sweep, side, sender]
                pltpu.make_async_remote_copy(
                    src_ref=slot, dst_ref=slot, send_sem=r_send.at[sweep, side, d],
                    recv_sem=r_recv.at[sweep, side, d],
                    device_id=(lax.rem(grp + 1, n_grp), fold), device_id_type=MESH).wait_recv()

    def whole_rows(read):
        parts = [read(f) for f in range(n_fold)]
        if rows % 16:
            return jnp.concatenate([part.astype(f32) for part in parts], axis=0).astype(bf16)
        return jnp.concatenate(parts, axis=0)

    def doubled(re, im):
        return jnp.concatenate(
            [jnp.concatenate([re, im], axis=1), jnp.concatenate([-im, re], axis=1)], axis=0)

    def build_local(sweep):
        def pair(h, carry):
            chunks = [whole_rows(lambda f, i=i: gath[sweep, f, 2 * h + i]) for i in range(2)]
            (are, aim), (bre, bim) = [(c[:, :128], c[:, 128:]) for c in chunks]
            local_rhs[0, 2 * h] = doubled(are, aim)
            local_rhs[0, 2 * h + 1] = doubled(bre, bim)
            left = jnp.concatenate([jnp.concatenate([are, aim, bre, bim], axis=0),
                                    jnp.concatenate([bre, bim, are, aim], axis=0)], axis=1)
            moved = jnp.dot(left, moves[...], preferred_element_type=f32).astype(bf16)
            for i in range(2):
                for hop in range(4):
                    cut = moved[2 * comps * i:2 * comps * (i + 1), 128 * hop:128 * hop + 128]
                    local_rhs[1 + hop, 2 * h + i] = doubled(cut[:comps], cut[comps:])
            return carry

        lax.fori_loop(0, HALF, pair, 0)

    row_site = lax.broadcasted_iota(jnp.int32, (rows * CHUNK, 256), 0) % CHUNK
    lane_site = lax.broadcasted_iota(jnp.int32, (rows * CHUNK, 256), 1) % CHUNK

    def same_site(product):
        kept = jnp.where(row_site == lane_site, product, 0.0)
        return jnp.sum(kept.reshape(rows, CHUNK, 256), axis=1)

    def apply_local():
        def chunk(g, carry):
            plane, x, low = g // HALF * HALF, g % HALF // 2, g % 2
            ahead, behind = plane + (x + 1) % 4 * 2 + low, plane + (x + 3) % 4 * 2 + low
            rhs = jnp.concatenate(
                [local_rhs[0, g], local_rhs[0, ahead], local_rhs[0, behind]]
                + [local_rhs[1 + hop, g] for hop in range(4)], axis=0)
            image[g] = same_site(jnp.dot(w_local[g], rhs, preferred_element_type=f32))
            return carry

        lax.fori_loop(0, GROUPS, chunk, 0)

    def dots(a, r):
        are, aim, rre, rim = a[:, :128], a[:, 128:], r[:, :128], r[:, 128:]
        return are * rre + aim * rim, are * rim - aim * rre, are * are + aim * aim

    def apply_across(sweep):
        def plane_chunk(h, sums):
            after = whole_rows(lambda f: rims[sweep, 0, f, h])
            before = whole_rows(lambda f: rims[sweep, 1, f, h])
            after = doubled(after[:, :128], after[:, 128:])
            before = doubled(before[:, :128], before[:, 128:])
            inner, outer = local_rhs[0, h], local_rhs[0, h + HALF]
            up = (outer.astype(f32) * live + after.astype(f32) * (1.0 - live)).astype(bf16)
            first = same_site(jnp.dot(w_across[h], jnp.concatenate([up, before], axis=0),
                                      preferred_element_type=f32))
            second = same_site(jnp.dot(w_across[h + HALF], jnp.concatenate([after, inner], axis=0),
                                       preferred_element_type=f32))
            first = first + image[h]
            second = (second + image[h + HALF]) * live
            image[h] = first
            image[h + HALF] = second
            one, two = dots(first, res[h]), dots(second, res[h + HALF])
            return tuple(s + a + b for s, a, b in zip(sums, one, two))

        zero = jnp.zeros((rows, 128), f32)
        return lax.fori_loop(0, HALF, plane_chunk, (zero, zero, zero))

    row8 = lax.broadcasted_iota(jnp.int32, (8, 128), 0)
    lane8 = lax.broadcasted_iota(jnp.int32, (8, 128), 1)

    def reduce_all(sweep, sums):
        re, im, norm = [jnp.sum(s, axis=0, keepdims=True) for s in sums]
        red[sweep, 0] = jnp.where(row8 == 0, re, jnp.where(row8 == 1, im, norm))

        def send(d, carry):
            pltpu.make_async_remote_copy(
                src_ref=red.at[sweep, 0], dst_ref=red.at[sweep, d],
                send_sem=s_send.at[sweep], recv_sem=s_recv.at[sweep],
                device_id=device(lax.rem(me + d, total)), device_id_type=MESH).start()
            return carry

        lax.fori_loop(1, total, send, 0)
        everyone = red.at[sweep, pl.ds(1, total - 1)]
        pltpu.make_async_copy(everyone, everyone, s_recv.at[sweep]).wait()
        value = jnp.sum(red[sweep], axis=0)
        for step in (4, 2, 1):
            value = value + jnp.where(lane8 // step % 2 == 0,
                                      pltpu.roll(value, 128 - step, 1), pltpu.roll(value, step, 1))
        real = lane8[:1] < 8 * nrhs
        norm = jnp.where(real, value[2:3], 1.0)
        pltpu.make_async_copy(everyone, everyone, s_send.at[sweep]).wait()
        return value[0:1] / norm, value[1:2] / norm

    def turned(alpha_re, alpha_im, v):
        re, im = v[:, :128], v[:, 128:]
        return jnp.concatenate([alpha_re * re - alpha_im * im, alpha_re * im + alpha_im * re], axis=1)

    for sweep in range(SWEEPS):
        gathers, edges = send_parts(sweep)
        if sweep == 0:
            for m in range(9):
                loads[m].wait()
                place = LOCAL.index(m) if m in LOCAL else ACROSS.index(m)
                target = w_local if m in LOCAL else w_across

                def two_rows(i, carry, m=m, place=place, target=target):
                    flipped = []
                    for a in range(2):
                        both = jnp.concatenate([raw[m, 0, 2 * i + a], raw[m, 1, 2 * i + a]], axis=0)
                        flipped.append(both.astype(f32).T)
                    for g in range(GROUPS):
                        piece = jnp.concatenate([f[8 * g:8 * g + 8] for f in flipped], axis=0)
                        target[g, pl.ds(pl.multiple_of(16 * i, 16), 16),
                               2 * comps * place:2 * comps * (place + 1)] = piece.astype(bf16)
                    return carry

                lax.fori_loop(0, rows // 2, two_rows, 0)
        wait_gather(sweep)
        build_local(sweep)
        apply_local()
        wait_edges(sweep)
        sums = apply_across(sweep)
        alpha_re, alpha_im = reduce_all(sweep, sums)

        def update(g, carry):
            r = res[g]
            step = turned(alpha_re, alpha_im, r)
            sol[g] = step if sweep == 0 else sol[g] + step
            res[g] = r - turned(alpha_re, alpha_im, image[g])
            return carry

        lax.fori_loop(0, GROUPS, update, 0)
        for copy in gathers + edges:
            copy.wait_send()

    for held, out in ((sol, sol_out), (res, res_out)):
        for p in range(2):
            chunks = [held[g, :, 128 * p:128 * p + 128] for g in range(GROUPS)]
            for k in range(nrhs):
                value = chunks[0] if k == 0 else pltpu.roll(chunks[0], -8 * k % 128, 1)
                for g in range(1, GROUPS):
                    shift = 8 * (g - k) % 128
                    moved = chunks[g] if shift == 0 else pltpu.roll(chunks[g], shift, 1)
                    value = jnp.where(lane // 8 == g, moved, value)
                out[p, k] = value


def body(n_grp, n_fold, blocks, source, plane_counts):
    rows, comps = blocks.shape[2], blocks.shape[3]
    nrhs = source.shape[2]
    bf16, f32 = jnp.bfloat16, jnp.float32
    shape = (2, nrhs, rows, GROUPS * CHUNK)
    vmem = pl.BlockSpec(memory_space=pltpu.VMEM)
    total = n_grp * n_fold
    outs = pl.pallas_call(
        functools.partial(kernel, n_grp, n_fold),
        out_shape=(jax.ShapeDtypeStruct(shape, f32), jax.ShapeDtypeStruct(shape, f32)),
        in_specs=[pl.BlockSpec(memory_space=pltpu.SMEM), pl.BlockSpec(memory_space=pl.ANY), vmem, vmem],
        out_specs=(vmem, vmem),
        scratch_shapes=[
            pltpu.VMEM(blocks.shape, bf16),
            pltpu.VMEM((GROUPS, rows * CHUNK, len(LOCAL) * 2 * comps), bf16),
            pltpu.VMEM((GROUPS, rows * CHUNK, len(ACROSS) * 2 * comps), bf16),
            pltpu.VMEM((GROUPS, rows, 256), f32),
            pltpu.VMEM((GROUPS, rows, 256), f32),
            pltpu.VMEM((GROUPS, rows, 256), f32),
            pltpu.VMEM((SWEEPS, n_fold, GROUPS, rows, 256), bf16),
            pltpu.VMEM((SWEEPS, HALF, rows, 256), bf16),
            pltpu.VMEM((SWEEPS, 2, n_fold, HALF, rows, 256), bf16),
            pltpu.VMEM((5, GROUPS, 2 * comps, 256), bf16),
            pltpu.VMEM((SWEEPS, total, 8, 128), f32),
            pltpu.SemaphoreType.DMA((9,)),
            pltpu.SemaphoreType.DMA((SWEEPS, n_fold)),
            pltpu.SemaphoreType.DMA((SWEEPS, n_fold)),
            pltpu.SemaphoreType.DMA((SWEEPS, 2, n_fold)),
            pltpu.SemaphoreType.DMA((SWEEPS, 2, n_fold)),
            pltpu.SemaphoreType.DMA((SWEEPS,)),
            pltpu.SemaphoreType.DMA((SWEEPS,)),
        ],
        compiler_params=pltpu.CompilerParams(
            collective_id=0, has_side_effects=True, vmem_limit_bytes=56 * 1024 * 1024),
    )(plane_counts, blocks, source.transpose(0, 2, 1, 3), lane_moves())
    return tuple(out.transpose(0, 2, 1, 3) for out in outs)


def solution(mesh):
    return jax.shard_map(
        functools.partial(body, mesh.shape["grp"], mesh.shape["fold"]),
        mesh=mesh,
        in_specs=(P(None, None, "fold", None, "grp"), P(None, "fold", None, "grp"), P("grp")),
        out_specs=(P(None, "fold", None, "grp"), P(None, "fold", None, "grp")),
        check_vma=False,
    )
```

time: 256 us -> 69 us (0.27); the launches traced: 252 us -> 68.8 us
  blocking collectives: 89.1 us -> 0 us
  Pallas kernels: 0 us -> 63.9 us
  local copies, waits for them, and re-layouts: 61 us -> 3.53 us
  other arithmetic: 43.7 us -> 0 us
  matrix products: 28.3 us -> 0 us
  waiting for transfers between devices: 15 us -> 0 us
  starting transfers between devices: 12.7 us -> 0 us
    psum x2 -> x0, blocking collectives: 84.8 us -> none  [body(): lax.psum((intersection_re, intersection_im, image_norm), ('grp', 'fold'))]
    pallas_call x0 -> x1, Pallas kernels: none -> 63.9 us  [body(): pl.pallas_call(functools.partial(kernel, n_grp, n_fold), out_shape=(jax.S...]
    unnamed x27 -> x2, local copies, waits for them, and re-layouts: 37.3 us -> 3.53 us
    dot_general x2 -> x0, matrix products: 28.3 us -> none  [stencil_apply(): jnp.einsum('mjrcs,mjpcks->prks', blocks, operand, preferred_element_type=...]
    another operation x2 -> x0, other arithmetic: 19.2 us -> none  [stencil_apply(): operand = jnp.stack([stacked, swapped], axis=1)]
    ppermute x4 -> x0, waiting for transfers between devices: 15 us -> none  [the longest x2 13.6 us: extended_2(): before = lax.ppermute(last, axis, up)]
    ppermute x4 -> x0, starting transfers between devices: 12.7 us -> none  [the longest x2 7.46 us: extended_2(): after = lax.ppermute(first, axis, down)]
    slice x22 -> x0, local copies, waits for them, and re-layouts: 11.3 us -> none  [the longest x4 3.55 us: hop_vectors(): neighbours.append(jnp.roll(lattice, 1, 6).reshape(flat_shape))]
  transfers between devices with their start and end apart: 4 -> 0, of which waited for: 2 -> 0; matrix products, arithmetic and copies ran while one was open for 11% -> 0% of each run, Pallas kernels for 0% -> 0%
where the time goes in v1:
time: 69 us; the launch traced here: 68.8 us
  Pallas kernels  63.9 us (93%)
  local copies, waits for them, and re-layouts  3.53 us (5%)
  between operations  1.29 us (2%)
    pallas_call x1, Pallas kernels, body(): pl.pallas_call(functools.partial(kernel, n_grp, n_fold), out_shape=(jax.S...  63.9 us
    unnamed x2, local copies, waits for them, and re-layouts  3.53 us

profile of v1, /device:TPU:0, one launch (start us, length us, event | category | flops | bytes accessed | tf_op | source)
XLA Modules:
  0.0 68.8 jit_solution(8304979732307371510)
XLA Ops:
  1.3 63.9 %shard_map.59 = (f32[2,12,32,128]{3,2,1,0:T(8,128)}, f32[2,12,32,128]{3,2,1,0:T(8,128)}) custom-call(s32[1]{0:T(128)S(6)} %copy.8.counts, bf16[9,2,32,64,128]{4,3,2,1,0:T(8,128)(2,1)} %blocks.1, bf16[2,12,32,128]{3,2,1,0:T(8,128)(2,1)} %bitcast.5, bf16[256,512]{1,0:T(8,128)(2,1)} %constant.2.clone.moves), custom_call_target="tpu_custom_call" | custom-call | tf_op jit(solution)/shard_map/pallas_call | solution.py:279
  65.2 1.8 %copy.9 = f32[2,32,12,128]{3,1,2,0:T(8,128)} copy(f32[2,32,12,128]{3,1,2,0:T(8,128)} %bitcast.4) | data formatting | bytes 786432
  67.0 1.8 %copy.10 = f32[2,32,12,128]{3,1,2,0:T(8,128)} copy(f32[2,32,12,128]{3,1,2,0:T(8,128)} %bitcast.3) | data formatting | bytes 786432

commit v2 on v1

--- a/solution.py
+++ b/solution.py
@@ -29,8 +29,8 @@
     return jnp.asarray(moves, jnp.bfloat16)
 
 
-def kernel(n_grp, n_fold, counts, blocks, source, moves, sol_out, res_out,
-           raw, w_local, w_across, res, sol, image, gath, last, rims, local_rhs, red,
+def kernel(n_grp, n_fold, counts, blocks, source, moves, sol, res,
+           raw, w_local, w_across, image, gath, last, rims, local_rhs, red,
            load_sem, x_send, x_recv, r_send, r_recv, s_send, s_recv):
     bf16, f32 = jnp.bfloat16, jnp.float32
     rows, comps = blocks.shape[2], blocks.shape[3]
@@ -78,7 +78,7 @@
             last[sweep, h] = (upper * live + lower * (1.0 - live)).astype(bf16)
             return carry
 
-        lax.fori_loop(0, HALF, fill, 0)
+        lax.fori_loop(0, HALF, fill, 0, unroll=2)
         gathers, edges = [], []
         for d in range(1, n_fold):
             gathers.append(pltpu.make_async_remote_copy(
@@ -142,7 +142,7 @@
                     local_rhs[1 + hop, 2 * h + i] = doubled(cut[:comps], cut[comps:])
             return carry
 
-        lax.fori_loop(0, HALF, pair, 0)
+        lax.fori_loop(0, HALF, pair, 0, unroll=2)
 
     row_site = lax.broadcasted_iota(jnp.int32, (rows * CHUNK, 256), 0) % CHUNK
     lane_site = lax.broadcasted_iota(jnp.int32, (rows * CHUNK, 256), 1) % CHUNK
@@ -161,7 +161,7 @@
             image[g] = same_site(jnp.dot(w_local[g], rhs, preferred_element_type=f32))
             return carry
 
-        lax.fori_loop(0, GROUPS, chunk, 0)
+        lax.fori_loop(0, GROUPS, chunk, 0, unroll=4)
 
     def dots(a, r):
         are, aim, rre, rim = a[:, :128], a[:, 128:], r[:, :128], r[:, 128:]
@@ -187,7 +187,7 @@
             return tuple(s + a + b for s, a, b in zip(sums, one, two))
 
         zero = jnp.zeros((rows, 128), f32)
-        return lax.fori_loop(0, HALF, plane_chunk, (zero, zero, zero))
+        return lax.fori_loop(0, HALF, plane_chunk, (zero, zero, zero), unroll=2)
 
     row8 = lax.broadcasted_iota(jnp.int32, (8, 128), 0)
     lane8 = lax.broadcasted_iota(jnp.int32, (8, 128), 1)
@@ -231,14 +231,14 @@
                     flipped = []
                     for a in range(2):
                         both = jnp.concatenate([raw[m, 0, 2 * i + a], raw[m, 1, 2 * i + a]], axis=0)
-                        flipped.append(both.astype(f32).T)
+                        flipped.append(both.T.astype(f32))
                     for g in range(GROUPS):
                         piece = jnp.concatenate([f[8 * g:8 * g + 8] for f in flipped], axis=0)
                         target[g, pl.ds(pl.multiple_of(16 * i, 16), 16),
                                2 * comps * place:2 * comps * (place + 1)] = piece.astype(bf16)
                     return carry
 
-                lax.fori_loop(0, rows // 2, two_rows, 0)
+                lax.fori_loop(0, rows // 2, two_rows, 0, unroll=4)
         wait_gather(sweep)
         build_local(sweep)
         apply_local()
@@ -253,10 +253,14 @@
             res[g] = r - turned(alpha_re, alpha_im, image[g])
             return carry
 
-        lax.fori_loop(0, GROUPS, update, 0)
+        lax.fori_loop(0, GROUPS, update, 0, unroll=4)
         for copy in gathers + edges:
             copy.wait_send()
 
+
+def finish(sol, res, sol_out, res_out):
+    nrhs = sol_out.shape[1]
+    lane = lax.broadcasted_iota(jnp.int32, (sol.shape[1], 128), 1)
     for held, out in ((sol, sol_out), (res, res_out)):
         for p in range(2):
             chunks = [held[g, :, 128 * p:128 * p + 128] for g in range(GROUPS)]
@@ -276,17 +280,16 @@
     shape = (2, nrhs, rows, GROUPS * CHUNK)
     vmem = pl.BlockSpec(memory_space=pltpu.VMEM)
     total = n_grp * n_fold
-    outs = pl.pallas_call(
+    held = jax.ShapeDtypeStruct((GROUPS, rows, 256), f32)
+    iterate = pl.pallas_call(
         functools.partial(kernel, n_grp, n_fold),
-        out_shape=(jax.ShapeDtypeStruct(shape, f32), jax.ShapeDtypeStruct(shape, f32)),
+        out_shape=(held, held),
         in_specs=[pl.BlockSpec(memory_space=pltpu.SMEM), pl.BlockSpec(memory_space=pl.ANY), vmem, vmem],
         out_specs=(vmem, vmem),
         scratch_shapes=[
             pltpu.VMEM(blocks.shape, bf16),
             pltpu.VMEM((GROUPS, rows * CHUNK, len(LOCAL) * 2 * comps), bf16),
             pltpu.VMEM((GROUPS, rows * CHUNK, len(ACROSS) * 2 * comps), bf16),
-            pltpu.VMEM((GROUPS, rows, 256), f32),
-            pltpu.VMEM((GROUPS, rows, 256), f32),
             pltpu.VMEM((GROUPS, rows, 256), f32),
             pltpu.VMEM((SWEEPS, n_fold, GROUPS, rows, 256), bf16),
             pltpu.VMEM((SWEEPS, HALF, rows, 256), bf16),
@@ -304,6 +307,12 @@
         compiler_params=pltpu.CompilerParams(
             collective_id=0, has_side_effects=True, vmem_limit_bytes=56 * 1024 * 1024),
     )(plane_counts, blocks, source.transpose(0, 2, 1, 3), lane_moves())
+    outs = pl.pallas_call(
+        finish,
+        out_shape=(jax.ShapeDtypeStruct(shape, f32), jax.ShapeDtypeStruct(shape, f32)),
+        in_specs=[vmem, vmem],
+        out_specs=(vmem, vmem),
+    )(*iterate)
     return tuple(out.transpose(0, 2, 1, 3) for out in outs)
 
 

time: 69 us -> 57.1 us (0.83)
  Pallas kernels: 63.9 us -> 55.6 us
  local copies, waits for them, and re-layouts: 3.53 us -> 0 us
    pallas_call x1 -> x2, Pallas kernels: 63.9 us -> 55.6 us  [the longest x1 50.5 us: body(): pl.pallas_call(functools.partial(kernel, n_grp, n_fold), out_shape=(held,...]
    unnamed x2 -> x0, local copies, waits for them, and re-layouts: 3.53 us -> none
where the time goes in v2:
time: 57.1 us; the launch traced here: 56.9 us
  Pallas kernels  55.6 us (97%)
  between operations  1.28 us (2%)
    pallas_call x1, Pallas kernels, body(): pl.pallas_call(functools.partial(kernel, n_grp, n_fold), out_shape=(held,...  50.5 us
    pallas_call x1, Pallas kernels, body(): pl.pallas_call(finish, out_shape=(jax.ShapeDtypeStruct(shape, f32), jax.S...  5.07 us

profile of v2, /device:TPU:0, one launch (start us, length us, event | category | flops | bytes accessed | tf_op | source)
XLA Modules:
  0.0 56.9 jit_solution(14850289618202840951)
XLA Ops:
  1.3 50.5 %shard_map.59 = (f32[16,32,256]{2,1,0:T(8,128)}, f32[16,32,256]{2,1,0:T(8,128)}) custom-call(s32[1]{0:T(128)S(6)} %copy.6.counts, bf16[9,2,32,64,128]{4,3,2,1,0:T(8,128)(2,1)} %blocks.1, bf16[2,12,32,128]{3,2,1,0:T(8,128)(2,1)} %bitcast.3, bf16[256,512]{1,0:T(8,128)(2,1)} %constant.2.clone.moves), custom_call_target="tpu_custom_call" | custom-call | tf_op jit(solution)/shard_map/pallas_call | solution.py:284
  51.8 5.1 %shard_map.60 = (f32[2,12,32,128]{3,2,1,0:T(8,128)}, f32[2,12,32,128]{3,2,1,0:T(8,128)}) custom-call(f32[16,32,256]{2,1,0:T(8,128)} %get-tuple-element.6.sol, f32[16,32,256]{2,1,0:T(8,128)} %get-tuple-element.7.res), custom_call_target="tpu_custom_call" | custom-call | tf_op jit(solution)/shard_map/pallas_call | solution.py:310

commit v3 on v2

--- a/solution.py
+++ b/solution.py
@@ -85,17 +85,12 @@
                 src_ref=gath.at[sweep, fold], dst_ref=gath.at[sweep, fold],
                 send_sem=x_send.at[sweep, d], recv_sem=x_recv.at[sweep, d],
                 device_id=(grp, lax.rem(fold + d, n_fold)), device_id_type=MESH))
-        for d in range(n_fold):
-            other = lax.rem(fold + d, n_fold)
+        for side, src, step in ((0, gath.at[sweep, fold, pl.ds(0, HALF)], n_grp - 1), (1, last.at[sweep], 1)):
             edges.append(pltpu.make_async_remote_copy(
-                src_ref=gath.at[sweep, fold, pl.ds(0, HALF)], dst_ref=rims.at[sweep, 0, fold],
-                send_sem=r_send.at[sweep, 0, d], recv_sem=r_recv.at[sweep, 0, d],
-                device_id=(lax.rem(grp + n_grp - 1, n_grp), other), device_id_type=MESH))
-            edges.append(pltpu.make_async_remote_copy(
-                src_ref=last.at[sweep], dst_ref=rims.at[sweep, 1, fold],
-                send_sem=r_send.at[sweep, 1, d], recv_sem=r_recv.at[sweep, 1, d],
-                device_id=(lax.rem(grp + 1, n_grp), other), device_id_type=MESH))
-        for copy in gathers + edges:
+                src_ref=src, dst_ref=rims.at[sweep, side, fold],
+                send_sem=r_send.at[sweep, side, 0], recv_sem=r_recv.at[sweep, side, 0],
+                device_id=(lax.rem(grp + step, n_grp), fold), device_id_type=MESH))
+        for copy in edges + gathers:
             copy.start()
         return gathers, edges
 
@@ -107,15 +102,26 @@
                 src_ref=slot, dst_ref=slot, send_sem=x_send.at[sweep, d], recv_sem=x_recv.at[sweep, d],
                 device_id=(grp, lax.rem(fold + d, n_fold)), device_id_type=MESH).wait_recv()
 
+    def forward(sweep, side, d, sender):
+        slot = rims.at[sweep, side, sender]
+        return pltpu.make_async_remote_copy(
+            src_ref=slot, dst_ref=slot, send_sem=r_send.at[sweep, side, d],
+            recv_sem=r_recv.at[sweep, side, d],
+            device_id=(grp, lax.rem(fold + d, n_fold)), device_id_type=MESH)
+
+    def pass_edges(sweep, edges):
+        passed = []
+        for side in range(2):
+            edges[side].wait_recv()
+            passed += [forward(sweep, side, d, fold) for d in range(1, n_fold)]
+            for copy in passed[-(n_fold - 1):]:
+                copy.start()
+        return passed
+
     def wait_edges(sweep):
         for side in range(2):
-            for d in range(n_fold):
-                sender = lax.rem(fold + n_fold - d, n_fold)
-                slot = rims.at[sweep, side, sender]
-                pltpu.make_async_remote_copy(
-                    src_ref=slot, dst_ref=slot, send_sem=r_send.at[sweep, side, d],
-                    recv_sem=r_recv.at[sweep, side, d],
-                    device_id=(lax.rem(grp + 1, n_grp), fold), device_id_type=MESH).wait_recv()
+            for d in range(1, n_fold):
+                forward(sweep, side, d, lax.rem(fold + n_fold - d, n_fold)).wait_recv()
 
     def whole_rows(read):
         parts = [read(f) for f in range(n_fold)]
@@ -151,7 +157,7 @@
         kept = jnp.where(row_site == lane_site, product, 0.0)
         return jnp.sum(kept.reshape(rows, CHUNK, 256), axis=1)
 
-    def apply_local():
+    def apply_local(begin, end):
         def chunk(g, carry):
             plane, x, low = g // HALF * HALF, g % HALF // 2, g % 2
             ahead, behind = plane + (x + 1) % 4 * 2 + low, plane + (x + 3) % 4 * 2 + low
@@ -161,7 +167,7 @@
             image[g] = same_site(jnp.dot(w_local[g], rhs, preferred_element_type=f32))
             return carry
 
-        lax.fori_loop(0, GROUPS, chunk, 0, unroll=4)
+        lax.fori_loop(begin, end, chunk, 0, unroll=8)
 
     def dots(a, r):
         are, aim, rre, rim = a[:, :128], a[:, 128:], r[:, :128], r[:, 128:]
@@ -187,7 +193,7 @@
             return tuple(s + a + b for s, a, b in zip(sums, one, two))
 
         zero = jnp.zeros((rows, 128), f32)
-        return lax.fori_loop(0, HALF, plane_chunk, (zero, zero, zero), unroll=2)
+        return lax.fori_loop(0, HALF, plane_chunk, (zero, zero, zero), unroll=4)
 
     row8 = lax.broadcasted_iota(jnp.int32, (8, 128), 0)
     lane8 = lax.broadcasted_iota(jnp.int32, (8, 128), 1)
@@ -239,9 +245,13 @@
                     return carry
 
                 lax.fori_loop(0, rows // 2, two_rows, 0, unroll=4)
+            passed = pass_edges(sweep, edges)
         wait_gather(sweep)
         build_local(sweep)
-        apply_local()
+        apply_local(0, HALF)
+        if sweep > 0:
+            passed = pass_edges(sweep, edges)
+        apply_local(HALF, GROUPS)
         wait_edges(sweep)
         sums = apply_across(sweep)
         alpha_re, alpha_im = reduce_all(sweep, sums)
@@ -254,7 +264,7 @@
             return carry
 
         lax.fori_loop(0, GROUPS, update, 0, unroll=4)
-        for copy in gathers + edges:
+        for copy in gathers + edges + passed:
             copy.wait_send()
 
 

time: 57.1 us -> 50.7 us (0.89)
  Pallas kernels: 55.6 us -> 49.3 us
    pallas_call x1, Pallas kernels: 50.5 us -> 44.2 us  [body(): pl.pallas_call(functools.partial(kernel, n_grp, n_fold), out_shape=(held,...]
where the time goes in v3:
time: 50.7 us; the launch traced here: 50.6 us
  Pallas kernels  49.3 us (97%)
  between operations  1.28 us (3%)
    pallas_call x1, Pallas kernels, body(): pl.pallas_call(functools.partial(kernel, n_grp, n_fold), out_shape=(held,...  44.2 us
    pallas_call x1, Pallas kernels, body(): pl.pallas_call(finish, out_shape=(jax.ShapeDtypeStruct(shape, f32), jax.S...  5.07 us

profile of v3, /device:TPU:0, one launch (start us, length us, event | category | flops | bytes accessed | tf_op | source)
XLA Modules:
  0.0 50.6 jit_solution(17148842970554666862)
XLA Ops:
  1.3 44.2 %shard_map.59 = (f32[16,32,256]{2,1,0:T(8,128)}, f32[16,32,256]{2,1,0:T(8,128)}) custom-call(s32[1]{0:T(128)S(6)} %copy.6.counts, bf16[9,2,32,64,128]{4,3,2,1,0:T(8,128)(2,1)} %blocks.1, bf16[2,12,32,128]{3,2,1,0:T(8,128)(2,1)} %bitcast.3, bf16[256,512]{1,0:T(8,128)(2,1)} %constant.2.clone.moves), custom_call_target="tpu_custom_call" | custom-call | tf_op jit(solution)/shard_map/pallas_call | solution.py:294
  45.5 5.1 %shard_map.60 = (f32[2,12,32,128]{3,2,1,0:T(8,128)}, f32[2,12,32,128]{3,2,1,0:T(8,128)}) custom-call(f32[16,32,256]{2,1,0:T(8,128)} %get-tuple-element.6.sol, f32[16,32,256]{2,1,0:T(8,128)} %get-tuple-element.7.res), custom_call_target="tpu_custom_call" | custom-call | tf_op jit(solution)/shard_map/pallas_call | solution.py:320
